TPU v7x, 512 devices: a whole 4x4x16 slice. The times are simulated.
512 devices in a mesh: zero: 32 (over y, x, core), dp: 16 (over z).
Axes of the slice: x: 4, y: 4, z: 16, core: 2. Of those that a mesh axis runs over, the one named last changes fastest.
Arguments:
- grad_partial: bfloat16 [16, 14, 3584, 256], P('dp', None, 'zero'), may hold values from -150 to 150
- momentum: float32 [14, 3584, 256], P(None, 'zero'), may hold values from -150 to 150
- shapes: int32 [14, 2], replicated, may hold values from 128 to 3584, as said below
- owners: int32 [14], replicated, may hold values from 0 to 31, as said below
Outputs:
- new_momentum: float32 [14, 3584, 256], P(None, 'zero')
- update: bfloat16 [14, 3584, 256], P(None, 'zero')
- owner_norms: float32 [32, 1], P('zero')
Inputs may be any that keep to these rules, and one draw needn't show every extreme that they name: `shapes`: column 0 is a multiple of 16 from 1792 to 3584, column 1 a multiple of 8 from 128 to 256; some matrix is live in full. `owners`: each owner holds at most 1 matrix, and some owner holds 1.
All inputs are finite; a program needn't handle non-finite values.
Results may differ from a plain program's by a relative error of at most 0.03.
Values may be sent and summed in bfloat16 or wider, within the bound.
A program may use at most 64 MiB of HBM per device.

v0:
```python
import jax
import jax.numpy as jnp
from jax import lax
from jax.sharding import PartitionSpec as P

ITERS = 3


coef_a = 3.4445
coef_b = -4.775
coef_c = 2.0315
epsilon = 1e-07
momentum_decay = 0.95


def unchanged(value):
    return value


def newton(matrices, total_squares, total_gram):
    norms = jnp.sqrt(total_squares(jnp.sum(jnp.square(matrices.astype(jnp.float32)), axis=(1, 2))))
    state = (matrices.astype(jnp.float32) / (norms + epsilon)[:, None, None]).astype(jnp.bfloat16)
    for sweep in range(ITERS):
        gram = total_gram(
            jnp.einsum("bls,blt->bst", state, state, preferred_element_type=jnp.float32)
        ).astype(jnp.bfloat16)
        square = jnp.einsum("bst,btu->bsu", gram, gram, preferred_element_type=jnp.float32)
        poly = (coef_b * gram.astype(jnp.float32) + coef_c * square).astype(jnp.bfloat16)
        state = (
            coef_a * state.astype(jnp.float32)
            + jnp.einsum("bls,bst->blt", state, poly, preferred_element_type=jnp.float32)
        ).astype(jnp.bfloat16)
    return (state, norms)


def per_device(grad_partial, momentum, shapes, owners):
    zero_count = lax.axis_size("zero")
    zero_index = lax.axis_index("zero")
    mat_count, shard_rows, short_side = momentum.shape
    per_owner = (mat_count + zero_count - 1) // zero_count
    row_ids = zero_index * shard_rows + lax.broadcasted_iota(jnp.int32, (1, shard_rows, 1), 1)
    col_ids = lax.broadcasted_iota(jnp.int32, (1, 1, short_side), 2)
    live_mask = (row_ids < shapes[:, 0][:, None, None]) & (col_ids < shapes[:, 1][:, None, None])
    summed = lax.psum(grad_partial[0].astype(jnp.float32).astype(jnp.bfloat16), "dp").astype(
        jnp.float32
    )
    gradient = jnp.where(live_mask, summed, 0.0)
    new_momentum = jnp.where(live_mask, momentum_decay * momentum + gradient, 0.0)
    nesterov = (gradient + momentum_decay * new_momentum).astype(jnp.bfloat16)
    index_ids = jnp.arange(mat_count, dtype=jnp.int32)
    slot_rank = jnp.sum(
        (owners[:, None] == owners[None, :]) & (index_ids[None, :] < index_ids[:, None]), axis=1
    )
    slot_ids = jnp.arange(zero_count * per_owner, dtype=jnp.int32)
    chosen = (owners[None, :] == slot_ids[:, None] // per_owner) & (
        slot_rank[None, :] == slot_ids[:, None] % per_owner
    )
    selector = chosen.astype(jnp.bfloat16)
    outgoing = jnp.einsum(
        "pk,krs->prs", selector, nesterov, preferred_element_type=jnp.float32
    ).astype(jnp.bfloat16)
    outgoing = outgoing.reshape(zero_count, per_owner, shard_rows, short_side)
    finals, norms = newton(
        lax.all_to_all(outgoing, "zero", split_axis=0, concat_axis=2, tiled=True)[0],
        unchanged,
        unchanged,
    )
    returned = lax.all_to_all(finals[None], "zero", split_axis=2, concat_axis=0, tiled=True)
    gathered, norms = (returned, norms[None, :])
    shards = jnp.einsum(
        "pk,prs->krs",
        selector,
        gathered.reshape(zero_count * per_owner, shard_rows, short_side),
        preferred_element_type=jnp.float32,
    )
    scale_factor = 0.2 * jnp.sqrt(jnp.maximum(shapes[:, 0], shapes[:, 1]).astype(jnp.float32))
    update = (shards * scale_factor[:, None, None]).astype(jnp.bfloat16)
    live_area = (shapes[:, 0] * shapes[:, 1]).astype(jnp.float32)
    slot_area = jnp.sum(jnp.where(chosen, live_area[None, :], 0.0), axis=1).reshape(
        zero_count, per_owner
    )
    my_area = lax.dynamic_slice_in_dim(slot_area, zero_index, 1, 0)
    owner_norms = jnp.where(my_area > 0.0, norms / jnp.sqrt(jnp.maximum(my_area, 1.0)), 0.0)
    return (new_momentum, update, owner_norms)


def solution(mesh):
    in_specs = (P("dp", None, "zero", None), P(None, "zero", None), P(), P())
    out_specs = (P(None, "zero", None), P(None, "zero", None), P("zero", None))
    return jax.shard_map(
        per_device, mesh=mesh, in_specs=in_specs, out_specs=out_specs, check_vma=False
    )
```

profile of v0, /device:TPU:1, one launch (start us, length us, event | category | flops | bytes accessed | tf_op | source)
XLA Modules:
  0.0 300.7 jit_solution(4298651072988692585)
XLA Ops:
  7.2 0.0 all-reduce.2.cloned.1.call-start
  7.2 0.7 all-reduce.2.cloned.1.call-update
  7.9 0.9 convert_reduce_fusion
  8.8 0.8 slice_bitcast_fusion.1
  9.6 0.1 broadcast_compare_fusion
  9.7 0.1 iota_compare_fusion
  9.7 0.0 copy-start
  9.7 134.9 %all-reduce.2.cloned.1.call-done = bf16[14,112,256]{2,1,0:T(8,128)(2,1)} async-done(((bf16[14,112,256]{2,1,0:T(8,128)(2,1)}), bf16[14,112,256]{2,1,0:T(8,128)(2,1)}) %all-reduce.2.cloned.1.call-update) | async-done | bytes 802832 | tf_op jit(solution)/shard_map/psum | solution.py:44
  144.6 3.4 %add_convert_fusion = (bf16[14,112,256]{2,1,0:T(8,128)(2,1)S(1)}, f32[14,112,256]{2,1,0:T(8,128)}) fusion(bf16[14,112,256]{2,1,0:T(8,128)(2,1)} %all-reduce.2.cloned.1.call-done, pred[14,256]{1,0:T(8,128)(4,1)S(1)} %iota_compare_fusion, pred[14,112]{1,0:T(8,128)(4,1)S(1)} %broadcast_compare_fusion, f32[14,112,256]{2,1,0:T(8,128)} %param.5), kind=kLoop, calls=%fused_computation.19 | loop fusion | flops 3612672 | bytes 4822048 | tf_op jit(solution)/shard_map/convert_element_type | solution.py:49
  148.1 0.0 copy-done
  148.1 0.8 convert_bitcast_fusion
  148.9 1.0 copy.32
  149.9 42.2 %all_to_all.8 = bf16[32,1,112,256]{3,2,1,0:T(8,128)(2,1)S(1)} all-to-all(bf16[32,1,112,256]{3,2,1,0:T(8,128)(2,1)S(1)} %copy.32), channel_id=1, replica_groups=mesh['zero'=32,'dp'=16] {'zero'}, dimensions={0} | all-to-all | bytes 3670016 | tf_op jit(solution)/shard_map/all_to_all | solution.py:64
  192.1 1.5 fusion.4
  194.3 0.6 fusion.5
  195.0 0.7 fusion.21
  195.7 1.0 copy.34
  196.7 2.1 fusion
  198.8 2.7 convolution_convert_fusion.1
  201.5 2.9 fusion.1
  204.5 0.0 copy-start.2
  204.5 1.2 copy-done.2
  205.7 0.7 convolution_convert_fusion
  206.4 2.9 fusion.3
  209.3 22.0 %copy.48 = bf16[1,1,3584,256]{3,1,0,2:T(2,128)(2,1)} copy(bf16[1,1,3584,256]{3,2,1,0:T(8,128)(2,1)S(1)} %fusion.3) | data formatting | bytes 3670016 | tf_op jit(solution)/shard_map/broadcast_in_dim | solution.py:68
  231.3 0.5 broadcast.177
  231.8 19.3 %reduce.2 = bf16[3584,256]{1,0:T(8,128)(2,1)S(1)} reduce(bf16[3584,1,1,256]{3,2,1,0:T(2,128)(2,1)} %bitcast.54, bf16[]{:T(256)} %broadcast.177), dimensions={1,2}, to_apply=%bitcast.53.reduce_sub_computation | reduce | bytes 3670018
  251.2 1.5 reshape.253
  252.6 0.0 copy-start.1
  252.6 4.4 %all-to-all-start.1 = ((bf16[32,2,14336]{2,1,0:T(2,128)(2,1)}), bf16[32,2,14336]{2,1,0:T(2,128)(2,1)S(1)}, u32[]{:S(2)}, u32[]{:S(2)}) async-start(bf16[32,2,14336]{2,1,0:T(2,128)(2,1)} %reshape.253), calls=%async_computation.1 | async-start | bytes 3670016 | tf_op jit(solution)/shard_map/all_to_all | solution.py:68
  257.0 0.0 copy-done.1
  257.1 0.1 select_reduce_fusion
  257.1 0.6 dynamic-slice.3
  259.1 22.9 %all-to-all-done.1 = bf16[32,2,14336]{2,1,0:T(2,128)(2,1)S(1)} async-done(((bf16[32,2,14336]{2,1,0:T(2,128)(2,1)}), bf16[32,2,14336]{2,1,0:T(2,128)(2,1)S(1)}, u32[]{:S(2)}, u32[]{:S(2)}) %all-to-all-start.1) | async-done | bytes 1835040 | tf_op jit(solution)/shard_map/all_to_all | solution.py:68
  282.0 6.5 %reshape.254 = bf16[3584,1,1,256]{3,2,1,0:T(2,128)(2,1)} reshape(bf16[32,2,14336]{2,1,0:T(2,128)(2,1)S(1)} %all-to-all-done.1) | data formatting | bytes 3670016
  288.5 2.4 copy.38
  290.9 0.7 multiply_convert_fusion
  291.6 1.2 copy.37
  (4 shorter events, 0.0 us)
Async XLA Ops:
  7.2 137.5 %all-reduce.2.cloned.1.call-start = ((), (), s32[]{:S(2)}) async-start(), calls=%async_computation.2 | async-start | bytes 1605632 | tf_op jit(solution)/shard_map/psum | solution.py:44
  9.7 138.3 %copy-start = (s32[14]{0:T(128)S(1)}, s32[14]{0:T(128)}, u32[]{:S(2)}) copy-start(s32[14]{0:T(128)} %param.7) | copy-start | bytes 172
  204.5 1.3 copy-start.2
  252.6 4.4 %copy-start.1 = (s32[14,2]{0,1:T(2,128)S(1)}, s32[14,2]{0,1:T(2,128)}, u32[]{:S(2)}) copy-start(s32[14,2]{0,1:T(2,128)} %param.6) | copy-start | bytes 340
  252.6 29.4 %all-to-all-start.1 = ((bf16[32,2,14336]{2,1,0:T(2,128)(2,1)}), bf16[32,2,14336]{2,1,0:T(2,128)(2,1)S(1)}, u32[]{:S(2)}, u32[]{:S(2)}) async-start(bf16[32,2,14336]{2,1,0:T(2,128)(2,1)} %reshape.253), calls=%async_computation.1 | async-start | bytes 3670016 | tf_op jit(solution)/shard_map/all_to_all | solution.py:68
Sparse Core Ops, SparseCore 0:
  10.3 134.2 all-reduce.1
where the time goes:
time: 301 us
  waiting for transfers between devices  158 us (52%)
  blocking collectives  42.2 us (14%)
  local copies, waits for them, and re-layouts  38.7 us (13%)
  other arithmetic  26.1 us (9%)
  between operations  17.3 us (6%)
  matrix products  13.5 us (4%)
  starting transfers between devices  4.41 us (1%)
    psum x1, waiting for transfers between devices, per_device(): lax.psum(grad_partial[0].astype(jnp.float32).astype(jnp.bfloat16), 'dp')  135 us
    all_to_all x1, blocking collectives, per_device(): lax.all_to_all(outgoing, 'zero', split_axis=0, concat_axis=2, tiled=True)[0]  42.2 us
    all_to_all x1, waiting for transfers between devices, per_device(): lax.all_to_all(finals[None], 'zero', split_axis=2, concat_axis=0, tiled=T...  22.9 us
    broadcast_in_dim x1, local copies, waits for them, and re-layouts, per_device(): finals[None]  22 us
    unnamed x1, other arithmetic  19.3 us
    unnamed x11, local copies, waits for them, and re-layouts  13.3 us
    dot_general x3, matrix products, newton(): jnp.einsum('bls,bst->blt', state, poly, preferred_element_type=jnp.float32)  7.94 us
  transfers between devices with their start and end apart: 2, of which 2 were waited for; matrix products, arithmetic and copies ran while one was open for 1% of the time, Pallas kernels for 0%

commit v1 on v0

v1 whole, which is shorter than its diff:
```python
import functools

import jax
import jax.numpy as jnp
from jax import lax
from jax.experimental import pallas as pl
from jax.experimental.pallas import tpu as pltpu
from jax.sharding import PartitionSpec as P

ITERS = 3
coef_a = 3.4445
coef_b = -4.775
coef_c = 2.0315
epsilon = 1e-07
momentum_decay = 0.95

MESH = pl.DeviceIdType.MESH
F32, BF16 = jnp.float32, jnp.bfloat16

PARENT = {8: 6, 7: 6, 6: 4, 5: 4, 4: 2, 3: 2, 2: 0, 1: 0}
REDUCE_ORDER = (8, 7, 5, 6, 3, 4, 1, 2)
SIDES = (1, -1)
PARTS = ((0, 64, (8, 7)), (64, 48, (7, 8)))
EXTRA = 16


def children(node, reach):
    return [c for c in sorted(PARENT, reverse=True) if PARENT[c] == node and c <= reach]


def split(value):
    high = value.astype(BF16)
    return high, (value - high.astype(F32)).astype(BF16)


def dot(a, b):
    return jnp.dot(a, b, preferred_element_type=F32)


def kernel(
    mats, n_dp, n_zero, shapes_ref, owners_ref, grad_ref, mom_ref, sum_ref, upd_ref, norm_ref,
    grads, moms, sums, upds, arrived_a, arrived_b, outgoing_a, outgoing_b, nest, gram, slabs, whole,
    load_sem, store_sem, rs_send, rs_recv, ag_send, ag_recv, plane_send, plane_recv,
):
    layer = lax.axis_index("dp")
    me = lax.axis_index("zero")
    shard, short = grads.shape[1:]
    slab = short // n_zero
    arrived, outgoing = (arrived_a, arrived_b), (outgoing_a, outgoing_b)
    owner = layer < mats
    mine = jnp.minimum(layer, mats - 1)

    load_grads = pltpu.make_async_copy(grad_ref.at[0], grads, load_sem.at[0])
    load_grads.start()
    load_moms = pltpu.make_async_copy(mom_ref.at[mine], moms, load_sem.at[1])
    load_moms.start()

    def along(step):
        return lax.rem(layer + (step + n_dp), n_dp)

    barrier = pltpu.get_barrier_semaphore()
    hops = sorted({c - p for c, p in PARENT.items()})
    for hop in hops:
        for side in SIDES:
            pl.semaphore_signal(barrier, inc=1, device_id={"dp": along(side * hop)}, device_id_type=MESH)

    def greet(step, carry):
        pl.semaphore_signal(barrier, inc=1, device_id={"zero": lax.rem(me + step, n_zero)}, device_id_type=MESH)
        return carry

    lax.fori_loop(1, n_zero, greet, 0)
    load_grads.wait()
    load_moms.wait()
    pl.semaphore_wait(barrier, 2 * len(hops) + n_zero - 1)

    def reduce_copy(part, s, node, source):
        return pltpu.make_async_remote_copy(
            src_ref=source,
            dst_ref=arrived[part].at[s, node],
            send_sem=rs_send.at[part, s, node],
            recv_sem=rs_recv.at[part, s, node],
            device_id={"dp": along(SIDES[s] * (node - PARENT[node]))},
            device_id_type=MESH,
        )

    def own_rows(part, j):
        first, rows, _ = PARTS[part]
        return grads.at[j, pl.ds(first, rows)]

    def collected(part, s, node, total):
        for child in children(node, PARTS[part][2][s]):
            reduce_copy(part, s, child, arrived[part].at[s, child]).wait_recv()
            total = total + arrived[part][s, child].astype(F32)
        return total

    def reduce_source(part, s, node, j):
        if children(node, PARTS[part][2][s]):
            return outgoing[part].at[s, node]
        return own_rows(part, j)

    for node in REDUCE_ORDER:
        for s, side in enumerate(SIDES):
            j = along(side * node)

            @pl.when(j < mats)
            def _():
                for part in range(len(PARTS)):
                    if node > PARTS[part][2][s]:
                        continue
                    if children(node, PARTS[part][2][s]):
                        total = collected(part, s, node, own_rows(part, j)[...].astype(F32))
                        outgoing[part][s, node] = total.astype(BF16)
                    reduce_copy(part, s, node, reduce_source(part, s, node, j)).start()

    def spread_copy(which, buffer, part, s, node, j):
        first, rows, _ = PARTS[part]
        if which == 1 and part == len(PARTS) - 1:
            rows += EXTRA
        window = buffer.at[j, pl.ds(first, rows)]
        return pltpu.make_async_remote_copy(
            src_ref=window,
            dst_ref=window,
            send_sem=ag_send.at[which, part, s, node],
            recv_sem=ag_recv.at[which, part, s, node],
            device_id={"dp": along(SIDES[s] * (node - PARENT[node]))},
            device_id_type=MESH,
        )

    def spread_from(which, buffer, part, s, node, j):
        for child in children(node, PARTS[part][2][s]):
            spread_copy(which, buffer, part, s, child, j).start()

    def spread_start(which, buffer):
        for part in range(len(PARTS)):
            for s in range(2):
                spread_from(which, buffer, part, s, 0, layer)

    def spread_forward(which, buffer, nodes):
        for node in nodes:
            for s, side in enumerate(SIDES):
                j = along(-side * node)

                @pl.when(j < mats)
                def _():
                    for part in range(len(PARTS)):
                        if node > PARTS[part][2][s]:
                            continue
                        spread_copy(which, buffer, part, s, node, j).wait_recv()
                        spread_from(which, buffer, part, s, node, j)

    def spread_sent(which, buffer):
        for node in PARENT:
            for s, side in enumerate(SIDES):
                j = along(-side * PARENT[node])

                @pl.when(j < mats)
                def _():
                    for part in range(len(PARTS)):
                        if node <= PARTS[part][2][s]:
                            spread_copy(which, buffer, part, s, node, j).wait_send()

    def plane_copy(source, target, which, peer):
        return pltpu.make_async_remote_copy(
            src_ref=source,
            dst_ref=target,
            send_sem=plane_send.at[which],
            recv_sem=plane_recv.at[which],
            device_id={"zero": peer},
            device_id_type=MESH,
        )

    def slab_of(ref, index):
        return ref.at[pl.ds(pl.multiple_of(index * slab, slab), slab)]

    def plane_wait(which):
        view = whole.at[pl.ds(0, short - slab)]
        return plane_copy(view, view, which, lax.rem(me + 1, n_zero))

    @pl.when(owner)
    def _():
        row_ids = me * shard + lax.broadcasted_iota(jnp.int32, (shard, short), 0)
        col_ids = lax.broadcasted_iota(jnp.int32, (shard, short), 1)
        live = (row_ids < shapes_ref[mine, 0]) & (col_ids < shapes_ref[mine, 1])
        totals = []
        for part in range(len(PARTS)):
            total = own_rows(part, layer)[...].astype(F32)
            for s in range(2):
                total = collected(part, s, 0, total)
            totals.append(total)
        gradient = jnp.where(live, jnp.concatenate(totals, axis=0), 0.0)
        sums[layer] = gradient.astype(BF16)
        spread_start(0, sums)
        new_momentum = jnp.where(live, momentum_decay * moms[...] + gradient, 0.0)
        nesterov = (gradient + momentum_decay * new_momentum).astype(BF16)
        nest[0:shard] = nesterov
        nest[shard:] = jnp.zeros((nest.shape[0] - shard, short), BF16)
        tall = nest[...]
        gram[...] = lax.dot_general(tall, tall, (((0,), (0,)), ((), ())), preferred_element_type=F32)

        def send(step, carry):
            peer = lax.rem(me + step, n_zero)
            plane_copy(slab_of(gram, peer), slabs.at[me], 0, peer).start()
            return carry

        lax.fori_loop(1, n_zero, send, 0)
        slabs[me] = slab_of(gram, me)[...]

    spread_forward(0, sums, (2, 1))

    @pl.when(owner)
    def _():
        plane_wait(0).wait_recv()
        total = jnp.sum(slabs[...], axis=0)
        slab_of(whole, me)[...] = total

        def send(step, carry):
            plane_copy(slab_of(whole, me), slab_of(whole, me), 1, lax.rem(me + step, n_zero)).start()
            return carry

        lax.fori_loop(1, n_zero, send, 0)

    spread_forward(0, sums, (4, 3, 6, 5))

    @pl.when(owner)
    def _():
        plane_wait(1).wait_recv()
        full = whole[...]
        on_diagonal = lax.broadcasted_iota(jnp.int32, (short, short), 0) == lax.broadcasted_iota(
            jnp.int32, (short, short), 1
        )
        square = jnp.where(on_diagonal, full, 0.0)
        square = jnp.sum(jnp.sum(square, axis=0, keepdims=True), axis=1, keepdims=True)
        norm = jnp.sqrt(square)
        inverse = 1.0 / (norm + epsilon)
        a = full * (inverse * inverse)
        state = (nest[...].astype(F32) * inverse).astype(BF16)
        for sweep in range(ITERS):
            a_high, a_low = split(a)
            poly = (coef_b * a_high.astype(F32) + coef_c * dot(a_high, a_high)).astype(BF16)
            if sweep < ITERS - 1:
                half = coef_a * a + dot(a_high, poly) + dot(a_low, poly)
                half_high, half_low = split(half)
                a = coef_a * half + dot(poly, half_high) + dot(poly, half_low)
            state = (coef_a * state.astype(F32) + dot(state, poly)).astype(BF16)
        longest = jnp.maximum(shapes_ref[mine, 0], shapes_ref[mine, 1]).astype(F32)
        scale = 0.2 * jnp.sqrt(jnp.full((1, 1), longest, F32))
        upds[layer, 0:shard] = (state[0:shard].astype(F32) * scale).astype(BF16)
        one = jnp.broadcast_to(norm, (EXTRA, short))
        high, rest = split(one)
        low, rest = split(one - high.astype(F32))
        place = lax.broadcasted_iota(jnp.int32, (EXTRA, short), 0)
        upds[layer, shard:] = jnp.where(
            place == 0, high.astype(F32), jnp.where(place == 1, low.astype(F32), jnp.where(place == 2, rest.astype(F32), 0.0))
        ).astype(BF16)
        spread_start(1, upds)

    spread_forward(0, sums, (8, 7))
    store_sums = pltpu.make_async_copy(sums, sum_ref, store_sem.at[0])
    store_sums.start()

    spread_forward(1, upds, (2, 1, 4, 3, 6, 5, 8, 7))
    store_upds = pltpu.make_async_copy(upds.at[:, pl.ds(0, shard)], upd_ref, store_sem.at[1])
    store_upds.start()

    result = jnp.zeros((1, short), F32)
    for k in range(mats):
        area = (shapes_ref[k, 0] * shapes_ref[k, 1]).astype(F32)
        norm = jnp.sum(upds[k, shard:].astype(F32), axis=0, keepdims=True)
        held = jnp.full((1, short), owners_ref[k], jnp.int32) == me
        result = result + jnp.where(held, norm / jnp.sqrt(jnp.full((1, short), area, F32)), 0.0)
    norm_ref[...] = jnp.broadcast_to(result[:, 0:128], (8, 128))

    for node in PARENT:
        for s, side in enumerate(SIDES):
            j = along(side * node)

            @pl.when(j < mats)
            def _():
                for part in range(len(PARTS)):
                    if node <= PARTS[part][2][s]:
                        reduce_copy(part, s, node, reduce_source(part, s, node, j)).wait_send()

    spread_sent(0, sums)
    spread_sent(1, upds)

    @pl.when(owner)
    def _():
        plane_wait(0).wait_send()
        plane_wait(1).wait_send()

    store_sums.wait()
    store_upds.wait()


def per_device(n_dp, n_zero, grad_partial, momentum, shapes, owners):
    mats, shard, short = momentum.shape
    smem = pl.BlockSpec(memory_space=pltpu.SMEM)
    anywhere = pl.BlockSpec(memory_space=pl.ANY)
    slots = 9
    sums, update, norms = pl.pallas_call(
        functools.partial(kernel, mats, n_dp, n_zero),
        out_shape=(
            jax.ShapeDtypeStruct((mats, shard, short), BF16),
            jax.ShapeDtypeStruct((mats, shard, short), BF16),
            jax.ShapeDtypeStruct((8, 128), F32),
        ),
        in_specs=[smem, smem, anywhere, anywhere],
        out_specs=(anywhere, anywhere, pl.BlockSpec(memory_space=pltpu.VMEM)),
        scratch_shapes=[
            pltpu.VMEM((mats, shard, short), BF16),
            pltpu.VMEM((shard, short), F32),
            pltpu.VMEM((mats, shard, short), BF16),
            pltpu.VMEM((mats, shard + EXTRA, short), BF16),
            pltpu.VMEM((2, slots, PARTS[0][1], short), BF16),
            pltpu.VMEM((2, slots, PARTS[1][1], short), BF16),
            pltpu.VMEM((2, slots, PARTS[0][1], short), BF16),
            pltpu.VMEM((2, slots, PARTS[1][1], short), BF16),
            pltpu.VMEM((128, short), BF16),
            pltpu.VMEM((short, short), F32),
            pltpu.VMEM((n_zero, short // n_zero, short), F32),
            pltpu.VMEM((short, short), F32),
            pltpu.SemaphoreType.DMA((2,)),
            pltpu.SemaphoreType.DMA((2,)),
            pltpu.SemaphoreType.DMA((len(PARTS), 2, slots)),
            pltpu.SemaphoreType.DMA((len(PARTS), 2, slots)),
            pltpu.SemaphoreType.DMA((2, len(PARTS), 2, slots)),
            pltpu.SemaphoreType.DMA((2, len(PARTS), 2, slots)),
            pltpu.SemaphoreType.DMA((2,)),
            pltpu.SemaphoreType.DMA((2,)),
        ],
        compiler_params=pltpu.CompilerParams(
            collective_id=0, has_side_effects=True, vmem_limit_bytes=32 * 1024 * 1024
        ),
    )(shapes, owners, grad_partial, momentum)
    row_ids = lax.axis_index("zero") * shard + lax.broadcasted_iota(jnp.int32, (1, shard, 1), 1)
    col_ids = lax.broadcasted_iota(jnp.int32, (1, 1, short), 2)
    live = (row_ids < shapes[:, 0][:, None, None]) & (col_ids < shapes[:, 1][:, None, None])
    new_momentum = jnp.where(live, momentum_decay * momentum + sums.astype(F32), 0.0)
    return new_momentum, update, norms[0:1, 0:1]


def solution(mesh):
    in_specs = (P("dp", None, "zero", None), P(None, "zero", None), P(), P())
    out_specs = (P(None, "zero", None), P(None, "zero", None), P("zero", None))
    return jax.shard_map(
        functools.partial(per_device, mesh.shape["dp"], mesh.shape["zero"]),
        mesh=mesh, in_specs=in_specs, out_specs=out_specs, check_vma=False,
    )
```

time: 301 us -> 80.9 us (0.27)
  the two profiles are of different devices: /device:TPU:1 before, /device:TPU:8 now
where the time goes in v1:
time: 80.9 us; the launch traced here: 80.7 us
  Pallas kernels  72.2 us (89%)
  local copies, waits for them, and re-layouts  6.14 us (8%)
  other arithmetic  1.67 us (2%)
    pallas_call x1, Pallas kernels, per_device(): pl.pallas_call(functools.partial(kernel, mats, n_dp, n_zero), out_shape=(...  72.2 us
    unnamed x8, local copies, waits for them, and re-layouts  4.86 us

profile of v1, /device:TPU:8, one launch (start us, length us, event | category | flops | bytes accessed | tf_op | source)
XLA Modules:
  0.0 80.7 jit_solution(1661996973996540127)
XLA Ops:
  0.6 0.8 slice_bitcast_fusion.1
  1.4 0.1 broadcast_compare_fusion
  1.5 0.1 iota_compare_fusion
  1.6 0.8 copy.7.shapes_ref
  2.3 0.0 copy-start
  2.3 1.4 %copy-done = f32[14,112,256]{2,1,0:T(8,128)S(1)} copy-done((f32[14,112,256]{2,1,0:T(8,128)S(1)}, f32[14,112,256]{2,1,0:T(8,128)}, u32[]{:S(2)}) %copy-start) | copy-done | bytes 1605656
  3.7 0.0 copy-start.1
  3.7 1.1 %copy-done.1 = bf16[1,14,112,256]{3,2,1,0:T(8,128)(2,1)S(1)} copy-done((bf16[1,14,112,256]{3,2,1,0:T(8,128)(2,1)S(1)}, bf16[1,14,112,256]{3,2,1,0:T(8,128)(2,1)}, u32[]{:S(2)}) %copy-start.1) | copy-done | bytes 802840
  4.9 0.0 copy-start.2
  4.9 0.7 copy-done.2
  5.5 72.2 %shard_map.67 = (bf16[14,112,256]{2,1,0:T(8,128)(2,1)S(1)}, bf16[14,112,256]{2,1,0:T(8,128)(2,1)S(1)}, f32[8,128]{1,0:T(8,128)S(1)}) custom-call(s32[14,2]{1,0:T(8,128)S(1)} %copy.7.shapes_ref, s32[14]{0:T(128)S(1)} %copy-done.2, bf16[1,14,112,256]{3,2,1,0:T(8,128)(2,1)S(1)} %copy-done.1, f32[14,112,256]{2,1,0:T(8,128)S(1)} %copy-done), custom_call_target="tpu_custom_call" | custom-call | tf_op jit(solution)/shard_map/pallas_call | solution.py:300
  77.7 0.5 slice.14
  78.3 1.5 %add_select_fusion = f32[14,112,256]{2,1,0:T(8,128)} fusion(bf16[14,112,256]{2,1,0:T(8,128)(2,1)S(1)} %get-tuple-element.6, f32[14,112,256]{2,1,0:T(8,128)S(1)} %copy-done, pred[14,256]{1,0:T(8,128)(4,1)S(1)} %iota_compare_fusion, pred[14,112]{1,0:T(8,128)(4,1)S(1)} %broadcast_compare_fusion), kind=kLoop, calls=%fused_computation | loop fusion | flops 2007040 | bytes 4019232 | tf_op jit(solution)/shard_map/jit(_where)/select_n | solution.py:338
  79.8 0.9 %copy.9 = bf16[14,112,256]{2,1,0:T(8,128)(2,1)} copy(bf16[14,112,256]{2,1,0:T(8,128)(2,1)S(1)} %get-tuple-element.15) | data formatting | bytes 1605632
  (1 shorter events, 0.0 us)
Async XLA Ops:
  2.3 1.4 %copy-start = (f32[14,112,256]{2,1,0:T(8,128)S(1)}, f32[14,112,256]{2,1,0:T(8,128)}, u32[]{:S(2)}) copy-start(f32[14,112,256]{2,1,0:T(8,128)} %mom_ref.1) | copy-start | bytes 4816900
  3.7 1.1 %copy-start.1 = (bf16[1,14,112,256]{3,2,1,0:T(8,128)(2,1)S(1)}, bf16[1,14,112,256]{3,2,1,0:T(8,128)(2,1)}, u32[]{:S(2)}) copy-start(bf16[1,14,112,256]{3,2,1,0:T(8,128)(2,1)} %grad_ref.1) | copy-start | bytes 2408452
  4.9 0.7 copy-start.2

commit v2 on v1

v2 whole, which is shorter than its diff:
```python
import functools

import jax
import jax.numpy as jnp
from jax import lax
from jax.experimental import pallas as pl
from jax.experimental.pallas import tpu as pltpu
from jax.sharding import PartitionSpec as P

ITERS = 3
coef_a = 3.4445
coef_b = -4.775
coef_c = 2.0315
epsilon = 1e-07
momentum_decay = 0.95

MESH = pl.DeviceIdType.MESH
F32, BF16 = jnp.float32, jnp.bfloat16

PARENT = {8: 6, 7: 6, 6: 4, 5: 4, 4: 2, 3: 2, 2: 0, 1: 0}
SIDES = (1, -1)
PARTS = ((0, 64, (8, 7)), (64, 48, (7, 8)))
SIDE_X, SIDE_Y = 4, 4
EXTRA = 16


def children(node, reach):
    return [c for c in sorted(PARENT, reverse=True) if PARENT[c] == node and c <= reach]


def split(value):
    high = value.astype(BF16)
    return high, (value - high.astype(F32)).astype(BF16)


def dot(a, b):
    return jnp.dot(a, b, preferred_element_type=F32)


def plane_moves():
    def far(step, size):
        return min(step, size - step)

    moves = [(y, x, c) for y in range(SIDE_Y) for x in range(SIDE_X) for c in range(2)][1:]
    return sorted(moves, key=lambda m: -(far(m[0], SIDE_Y) + far(m[1], SIDE_X)))


def kernel(
    mats, n_dp, n_zero, shapes_ref, grad_ref, mom_ref, new_ref, upd_ref,
    grads, moms, sums, news, own, arrived_a, arrived_b, outgoing_a, outgoing_b, nest, gram, slabs, whole,
    load_sem, store_sem, met_sem, rs_send, rs_recv, ag_send, ag_recv, plane_send, plane_recv,
):
    layer = lax.axis_index("dp")
    me = lax.axis_index("zero")
    shard, short = grads.shape[1:]
    slab = short // n_zero
    arrived, outgoing = (arrived_a, arrived_b), (outgoing_a, outgoing_b)
    owner = layer < mats
    mine = jnp.minimum(layer, mats - 1)

    load_grads = pltpu.make_async_copy(grad_ref.at[0], grads, load_sem.at[0])
    load_grads.start()
    load_moms = pltpu.make_async_copy(mom_ref, moms, load_sem.at[1])
    load_moms.start()

    def along(step):
        return lax.rem(layer + (step + n_dp), n_dp)

    core, here_x, here_y = lax.rem(me, 2), lax.rem(me // 2, SIDE_X), me // (2 * SIDE_X)

    def beside(move):
        y, x, c = move
        there_y = lax.rem(here_y + (y + SIDE_Y), SIDE_Y)
        there_x = lax.rem(here_x + (x + SIDE_X), SIDE_X)
        return (there_y * SIDE_X + there_x) * 2 + lax.rem(core + c, 2)

    def greet(semaphore, where):
        pl.semaphore_signal(semaphore, inc=1, device_id=where, device_id_type=MESH)

    barrier = pltpu.get_barrier_semaphore()
    hops = sorted({c - p for c, p in PARENT.items()})
    for hop in hops:
        for side in SIDES:
            greet(barrier, {"dp": along(side * hop)})
    rows_x, rows_y, pair = ((0, 1, 0), (0, -1, 0)), ((1, 0, 0), (-1, 0, 0)), ((0, 0, 1),)
    for move in rows_x + rows_y + pair:
        greet(barrier, {"zero": beside(move)})
    load_grads.wait()
    pl.semaphore_wait(barrier, 2 * len(hops) + 5)
    rounds = (rows_x, pair, rows_y, ((1, 0, 0),))

    def meet(index):
        if index > 0:
            pl.semaphore_wait(met_sem.at[index - 1], len(rounds[index - 1]))
        if index < len(rounds):
            for move in rounds[index]:
                greet(met_sem.at[index], {"zero": beside(move)})

    meet(0)

    def reduce_copy(part, s, node, source):
        return pltpu.make_async_remote_copy(
            src_ref=source,
            dst_ref=arrived[part].at[s, node],
            send_sem=rs_send.at[part, s, node],
            recv_sem=rs_recv.at[part, s, node],
            device_id={"dp": along(SIDES[s] * (node - PARENT[node]))},
            device_id_type=MESH,
        )

    def own_rows(part, j):
        first, rows, _ = PARTS[part]
        return grads.at[j, pl.ds(first, rows)]

    def collected(part, s, node, total):
        for child in children(node, PARTS[part][2][s]):
            reduce_copy(part, s, child, arrived[part].at[s, child]).wait_recv()
            total = total + arrived[part][s, child].astype(F32)
        return total

    def reduce_source(part, s, node, j):
        if children(node, PARTS[part][2][s]):
            return outgoing[part].at[s, node]
        return own_rows(part, j)

    def reduce_step(node):
        for s, side in enumerate(SIDES):
            j = along(side * node)

            @pl.when(j < mats)
            def _():
                for part in range(len(PARTS)):
                    if node > PARTS[part][2][s]:
                        continue
                    if children(node, PARTS[part][2][s]):
                        total = collected(part, s, node, own_rows(part, j)[...].astype(F32))
                        outgoing[part][s, node] = total.astype(BF16)
                    reduce_copy(part, s, node, reduce_source(part, s, node, j)).start()

    for node in (8, 7, 5, 6):
        reduce_step(node)
    meet(1)
    for node in (3, 4):
        reduce_step(node)
    meet(2)
    for node in (1, 2):
        reduce_step(node)
    meet(3)

    def spread_copy(which, part, s, node, j):
        first, rows, _ = PARTS[part]
        if which == 1 and part == len(PARTS) - 1:
            rows += EXTRA
        window = (sums, upd_ref)[which].at[j, pl.ds(first, rows)]
        source = window
        if which == 1 and PARENT[node] == 0:
            source = own.at[pl.ds(first, rows)]
        return pltpu.make_async_remote_copy(
            src_ref=source,
            dst_ref=window,
            send_sem=ag_send.at[which, part, s, node],
            recv_sem=ag_recv.at[which, part, s, node],
            device_id={"dp": along(SIDES[s] * (node - PARENT[node]))},
            device_id_type=MESH,
        )

    def spread_step(which, node):
        for s, side in enumerate(SIDES):
            if node == 0 and s == 1:
                continue
            j = along(-side * node)

            @pl.when(j < mats)
            def _():
                sides = (0, 1) if node == 0 else (s,)
                last = []
                for part in range(len(PARTS)):
                    for t in sides:
                        reach = PARTS[part][2][t]
                        if node > reach:
                            continue
                        if node > 0:
                            spread_copy(which, part, t, node, j).wait_recv()
                        for child in children(node, reach):
                            copy = spread_copy(which, part, t, child, j)
                            if children(child, reach):
                                copy.start()
                            else:
                                last.append(copy)
                for copy in last:
                    copy.start()

    def spread_sent(which):
        for node in PARENT:
            for s, side in enumerate(SIDES):
                j = along(-side * PARENT[node])

                @pl.when(j < mats)
                def _():
                    for part in range(len(PARTS)):
                        if node <= PARTS[part][2][s]:
                            spread_copy(which, part, s, node, j).wait_send()

    def plane_copy(source, target, which, peer):
        return pltpu.make_async_remote_copy(
            src_ref=source,
            dst_ref=target,
            send_sem=plane_send.at[which],
            recv_sem=plane_recv.at[which],
            device_id={"zero": peer},
            device_id_type=MESH,
        )

    def slab_of(ref, index):
        return ref.at[pl.ds(pl.multiple_of(index * slab, slab), slab)]

    def plane_wait(which):
        view = whole.at[pl.ds(0, short - slab)]
        return plane_copy(view, view, which, lax.rem(me + 1, n_zero))

    row_ids = me * shard + lax.broadcasted_iota(jnp.int32, (shard, short), 0)
    col_ids = lax.broadcasted_iota(jnp.int32, (shard, short), 1)

    def live_part(j):
        return (row_ids < shapes_ref[0, j]) & (col_ids < shapes_ref[1, j])

    def new_momentum(j, gradient):
        news[j] = jnp.where(live_part(j), momentum_decay * moms[j] + gradient, 0.0)

    load_moms.wait()
    meet(4)

    @pl.when(owner)
    def _():
        totals = []
        for part in range(len(PARTS)):
            total = own_rows(part, layer)[...].astype(F32)
            for s in range(2):
                total = collected(part, s, 0, total)
            totals.append(total)
        live = live_part(mine)
        gradient = jnp.where(live, jnp.concatenate(totals, axis=0), 0.0)
        sums[layer] = gradient.astype(BF16)
        momentum = jnp.where(live, momentum_decay * moms[layer] + gradient, 0.0)
        nesterov = (gradient + momentum_decay * momentum).astype(BF16)
        nest[0:shard] = nesterov
        nest[shard:] = jnp.zeros((nest.shape[0] - shard, short), BF16)
        tall = nest[...]
        gram[...] = lax.dot_general(tall, tall, (((0,), (0,)), ((), ())), preferred_element_type=F32)
        for move in plane_moves():
            peer = beside(move)
            plane_copy(slab_of(gram, peer), slabs.at[me], 0, peer).start()
        slabs[me] = slab_of(gram, me)[...]

    spread_step(0, 0)
    spread_step(0, 2)

    @pl.when(owner)
    def _():
        plane_wait(0).wait_recv()
        slab_of(whole, me)[...] = jnp.sum(slabs[...], axis=0)
        for move in plane_moves():
            plane_copy(slab_of(whole, me), slab_of(whole, me), 1, beside(move)).start()

    spread_step(0, 4)

    @pl.when(owner)
    def _():
        plane_wait(1).wait_recv()
        full = whole[...]
        on_diagonal = lax.broadcasted_iota(jnp.int32, (short, short), 0) == lax.broadcasted_iota(
            jnp.int32, (short, short), 1
        )
        square = jnp.where(on_diagonal, full, 0.0)
        square = jnp.sum(jnp.sum(square, axis=0, keepdims=True), axis=1, keepdims=True)
        norm = jnp.sqrt(square)
        inverse = 1.0 / (norm + epsilon)
        a = full * (inverse * inverse)
        state = (nest[...].astype(F32) * inverse).astype(BF16)
        for sweep in range(ITERS):
            a_high, a_low = split(a)
            poly = (coef_b * a_high.astype(F32) + coef_c * dot(a_high, a_high)).astype(BF16)
            if sweep < ITERS - 1:
                half = coef_a * a + dot(a_high, poly) + dot(a_low, poly)
                half_high, half_low = split(half)
                a = coef_a * half + dot(poly, half_high) + dot(poly, half_low)
            state = (coef_a * state.astype(F32) + dot(state, poly)).astype(BF16)
        longest = jnp.maximum(shapes_ref[0, mine], shapes_ref[1, mine]).astype(F32)
        scale = 0.2 * jnp.sqrt(jnp.full((1, 1), longest, F32))
        own[0:shard] = (state[0:shard].astype(F32) * scale).astype(BF16)
        one = jnp.broadcast_to(norm, (EXTRA, short))
        high, rest = split(one)
        low, rest = split(one - high.astype(F32))
        place = lax.broadcasted_iota(jnp.int32, (EXTRA, short), 0)
        own[shard:] = jnp.where(
            place == 0, high.astype(F32), jnp.where(place == 1, low.astype(F32), jnp.where(place == 2, rest.astype(F32), 0.0))
        ).astype(BF16)

    spread_step(1, 0)
    keep = pltpu.make_async_copy(own, upd_ref.at[mine], store_sem.at[0])

    @pl.when(owner)
    def _():
        keep.start()

    def new_momenta(node):
        if node == 8:
            j = along(8)

            @pl.when(j < mats)
            def _():
                new_momentum(j, sums[j].astype(F32))
            return
        for s, side in enumerate(SIDES):
            if node == 0 and s == 1:
                continue
            j = along(-side * node)

            @pl.when(j < mats)
            def _():
                new_momentum(j, sums[j].astype(F32))

    spread_step(0, 6)
    spread_step(0, 1)
    for node in (0, 1, 2):
        new_momenta(node)
    spread_step(1, 2)
    spread_step(0, 3)
    for node in (3, 4):
        new_momenta(node)
    spread_step(1, 4)
    spread_step(0, 5)
    for node in (5, 6):
        new_momenta(node)
    spread_step(1, 6)
    for node in (7, 8):
        spread_step(0, node)
        new_momenta(node)
    store_news = pltpu.make_async_copy(news, new_ref, store_sem.at[1])
    store_news.start()

    for node in PARENT:
        for s, side in enumerate(SIDES):
            j = along(side * node)

            @pl.when(j < mats)
            def _():
                for part in range(len(PARTS)):
                    if node <= PARTS[part][2][s]:
                        reduce_copy(part, s, node, reduce_source(part, s, node, j)).wait_send()

    spread_sent(0)

    @pl.when(owner)
    def _():
        plane_wait(0).wait_send()
        plane_wait(1).wait_send()
        keep.wait()

    for node in (1, 3, 5, 7, 8):
        spread_step(1, node)
    spread_sent(1)
    store_news.wait()


def finish(mats, shapes_ref, owners_ref, new_in, upd_in, new_ref, upd_ref, norm_ref, tails, sem):
    shard, short = new_in.shape[1:]
    copies = (
        pltpu.make_async_copy(upd_in.at[:, pl.ds(shard, EXTRA)], tails, sem.at[0]),
        pltpu.make_async_copy(new_in, new_ref, sem.at[1]),
        pltpu.make_async_copy(upd_in.at[:, pl.ds(0, shard)], upd_ref, sem.at[2]),
    )
    for copy in copies:
        copy.start()
    me = lax.axis_index("zero")
    copies[0].wait()
    result = jnp.zeros((1, short), F32)
    for k in range(mats):
        area = (shapes_ref[0, k] * shapes_ref[1, k]).astype(F32)
        norm = jnp.sum(tails[k].astype(F32), axis=0, keepdims=True)
        held = jnp.full((1, short), owners_ref[k], jnp.int32) == me
        result = result + jnp.where(held, norm / jnp.sqrt(jnp.full((1, short), area, F32)), 0.0)
    norm_ref[...] = result[:, 0:1]
    copies[1].wait()
    copies[2].wait()


def per_device(n_dp, n_zero, grad_partial, momentum, shapes, owners):
    mats, shard, short = momentum.shape
    smem = pl.BlockSpec(memory_space=pltpu.SMEM)
    hbm = pl.BlockSpec(memory_space=pltpu.HBM)
    anywhere = pl.BlockSpec(memory_space=pl.ANY)
    slots = 9
    turned = pltpu.with_memory_space_constraint(shapes.T, pltpu.HBM)
    owners = pltpu.with_memory_space_constraint(owners, pltpu.HBM)
    new, update = pl.pallas_call(
        functools.partial(kernel, mats, n_dp, n_zero),
        out_shape=(
            jax.ShapeDtypeStruct((mats, shard, short), F32),
            jax.ShapeDtypeStruct((mats, shard + EXTRA, short), BF16),
        ),
        in_specs=[smem, hbm, hbm],
        out_specs=(anywhere, anywhere),
        scratch_shapes=[
            pltpu.VMEM((mats, shard, short), BF16),
            pltpu.VMEM((mats, shard, short), F32),
            pltpu.VMEM((mats, shard, short), BF16),
            pltpu.VMEM((mats, shard, short), F32),
            pltpu.VMEM((shard + EXTRA, short), BF16),
            pltpu.VMEM((2, slots, PARTS[0][1], short), BF16),
            pltpu.VMEM((2, slots, PARTS[1][1], short), BF16),
            pltpu.VMEM((2, slots, PARTS[0][1], short), BF16),
            pltpu.VMEM((2, slots, PARTS[1][1], short), BF16),
            pltpu.VMEM((128, short), BF16),
            pltpu.VMEM((short, short), F32),
            pltpu.VMEM((n_zero, short // n_zero, short), F32),
            pltpu.VMEM((short, short), F32),
            pltpu.SemaphoreType.DMA((2,)),
            pltpu.SemaphoreType.DMA((2,)),
            pltpu.SemaphoreType.REGULAR((4,)),
            pltpu.SemaphoreType.DMA((len(PARTS), 2, slots)),
            pltpu.SemaphoreType.DMA((len(PARTS), 2, slots)),
            pltpu.SemaphoreType.DMA((2, len(PARTS), 2, slots)),
            pltpu.SemaphoreType.DMA((2, len(PARTS), 2, slots)),
            pltpu.SemaphoreType.DMA((2,)),
            pltpu.SemaphoreType.DMA((2,)),
        ],
        compiler_params=pltpu.CompilerParams(
            collective_id=0, has_side_effects=True, vmem_limit_bytes=24 * 1024 * 1024
        ),
    )(turned, *(pltpu.with_memory_space_constraint(a, pltpu.HBM) for a in (grad_partial, momentum)))
    return pl.pallas_call(
        functools.partial(finish, mats),
        out_shape=(
            jax.ShapeDtypeStruct((mats, shard, short), F32),
            jax.ShapeDtypeStruct((mats, shard, short), BF16),
            jax.ShapeDtypeStruct((1, 1), F32),
        ),
        in_specs=[smem, smem, anywhere, anywhere],
        out_specs=(anywhere, anywhere, pl.BlockSpec(memory_space=pltpu.VMEM)),
        scratch_shapes=[pltpu.VMEM((mats, EXTRA, short), BF16), pltpu.SemaphoreType.DMA((3,))],
        compiler_params=pltpu.CompilerParams(vmem_limit_bytes=24 * 1024 * 1024),
    )(turned, owners, new, update)


def solution(mesh):
    in_specs = (P("dp", None, "zero", None), P(None, "zero", None), P(), P())
    out_specs = (P(None, "zero", None), P(None, "zero", None), P("zero", None))
    return jax.shard_map(
        functools.partial(per_device, mesh.shape["dp"], mesh.shape["zero"]),
        mesh=mesh, in_specs=in_specs, out_specs=out_specs, check_vma=False,
    )
```

time: 80.9 us -> 72.2 us (0.89)
  the two profiles are of different devices: /device:TPU:8 before, /device:TPU:1 now
where the time goes in v2:
time: 72.2 us; the launch traced here: 71.5 us
  Pallas kernels  70.8 us (98%)
    pallas_call x1, Pallas kernels, per_device(): pl.pallas_call(functools.partial(kernel, mats, n_dp, n_zero), out_shape=(...  68.2 us
    pallas_call x1, Pallas kernels, per_device(): pl.pallas_call(functools.partial(finish, mats), out_shape=(jax.ShapeDtype...  2.66 us

profile of v2, /device:TPU:1, one launch (start us, length us, event | category | flops | bytes accessed | tf_op | source)
XLA Modules:
  0.0 71.5 jit_solution(1828235789129614747)
XLA Ops:
  0.6 68.2 %shard_map.67 = (f32[14,112,256]{2,1,0:T(8,128)S(1)}, bf16[14,128,256]{2,1,0:T(8,128)(2,1)S(1)}) custom-call(s32[2,14]{1,0:T(2,128)} %bitcast.1, bf16[1,14,112,256]{3,2,1,0:T(8,128)(2,1)} %grad_ref.1, f32[14,112,256]{2,1,0:T(8,128)} %mom_ref.1), custom_call_target="tpu_custom_call" | custom-call | tf_op jit(solution)/shard_map/pallas_call | solution.py:396
  68.8 2.7 %shard_map.68 = (f32[14,112,256]{2,1,0:T(8,128)}, bf16[14,112,256]{2,1,0:T(8,128)(2,1)}, f32[1,1]{1,0:T(1,128)}) custom-call(s32[2,14]{1,0:T(2,128)} %bitcast.2, s32[14]{0:T(128)} %owners_ref.1, f32[14,112,256]{2,1,0:T(8,128)S(1)} %get-tuple-element.5.new_in, bf16[14,128,256]{2,1,0:T(8,128)(2,1)S(1)} %get-tuple-element.6.upd_in), custom_call_target="tpu_custom_call" | custom-call | tf_op jit(solution)/shard_map/pallas_call | solution.py:432

commit v3 on v2

--- a/solution.py
+++ b/solution.py
@@ -37,26 +37,35 @@
     return jnp.dot(a, b, preferred_element_type=F32)
 
 
-def plane_moves():
+def chip_moves():
     def far(step, size):
         return min(step, size - step)
 
-    moves = [(y, x, c) for y in range(SIDE_Y) for x in range(SIDE_X) for c in range(2)][1:]
+    moves = [(y, x) for y in range(SIDE_Y) for x in range(SIDE_X)]
     return sorted(moves, key=lambda m: -(far(m[0], SIDE_Y) + far(m[1], SIDE_X)))
 
 
 def kernel(
-    mats, n_dp, n_zero, shapes_ref, grad_ref, mom_ref, new_ref, upd_ref,
-    grads, moms, sums, news, own, arrived_a, arrived_b, outgoing_a, outgoing_b, nest, gram, slabs, whole,
+    mats, n_dp, n_zero, shapes_ref, owners_ref, grad_ref, mom_ref, new_ref, upd_ref, norm_ref,
+    grads, moms, sums, news, own, tails, arrived_a, arrived_b, outgoing_a, outgoing_b, nest, gram, slabs, whole,
     load_sem, store_sem, met_sem, rs_send, rs_recv, ag_send, ag_recv, plane_send, plane_recv,
 ):
     layer = lax.axis_index("dp")
     me = lax.axis_index("zero")
     shard, short = grads.shape[1:]
-    slab = short // n_zero
+    half_short = short // 2
+    slab = 3 * half_short // (SIDE_X * SIDE_Y)
     arrived, outgoing = (arrived_a, arrived_b), (outgoing_a, outgoing_b)
-    owner = layer < mats
-    mine = jnp.minimum(layer, mats - 1)
+    half = n_dp // 2
+
+    def held(at):
+        return (at - (half - 1)) * (at - half) != 0
+
+    def matrix(at):
+        return at - (n_dp - mats) * (at // half)
+
+    owner = held(layer)
+    mine = matrix(layer)
 
     load_grads = pltpu.make_async_copy(grad_ref.at[0], grads, load_sem.at[0])
     load_grads.start()
@@ -73,6 +82,13 @@
         there_y = lax.rem(here_y + (y + SIDE_Y), SIDE_Y)
         there_x = lax.rem(here_x + (x + SIDE_X), SIDE_X)
         return (there_y * SIDE_X + there_x) * 2 + lax.rem(core + c, 2)
+
+    adds = core == lax.rem(here_x + here_y, 2)
+
+    def adder(move):
+        y, x = lax.rem(here_y + move[0], SIDE_Y), lax.rem(here_x + move[1], SIDE_X)
+        chip = y * SIDE_X + x
+        return chip, chip * 2 + lax.rem(x + y, 2)
 
     def greet(semaphore, where):
         pl.semaphore_signal(semaphore, inc=1, device_id=where, device_id_type=MESH)
@@ -110,10 +126,10 @@
 
     def own_rows(part, j):
         first, rows, _ = PARTS[part]
-        return grads.at[j, pl.ds(first, rows)]
+        return grads.at[matrix(j), pl.ds(first, rows)]
 
     def collected(part, s, node, total):
-        for child in children(node, PARTS[part][2][s]):
+        for child in reversed(children(node, PARTS[part][2][s])):
             reduce_copy(part, s, child, arrived[part].at[s, child]).wait_recv()
             total = total + arrived[part][s, child].astype(F32)
         return total
@@ -124,14 +140,14 @@
         return own_rows(part, j)
 
     def reduce_step(node):
-        for s, side in enumerate(SIDES):
-            j = along(side * node)
-
-            @pl.when(j < mats)
-            def _():
-                for part in range(len(PARTS)):
-                    if node > PARTS[part][2][s]:
-                        continue
+        for part in range(len(PARTS)):
+            for s, side in enumerate(SIDES):
+                if node > PARTS[part][2][s]:
+                    continue
+                j = along(side * node)
+
+                @pl.when(held(j))
+                def _():
                     if children(node, PARTS[part][2][s]):
                         total = collected(part, s, node, own_rows(part, j)[...].astype(F32))
                         outgoing[part][s, node] = total.astype(BF16)
@@ -151,7 +167,7 @@
         first, rows, _ = PARTS[part]
         if which == 1 and part == len(PARTS) - 1:
             rows += EXTRA
-        window = (sums, upd_ref)[which].at[j, pl.ds(first, rows)]
+        window = (sums, upd_ref)[which].at[matrix(j), pl.ds(first, rows)]
         source = window
         if which == 1 and PARENT[node] == 0:
             source = own.at[pl.ds(first, rows)]
@@ -165,37 +181,28 @@
         )
 
     def spread_step(which, node):
-        for s, side in enumerate(SIDES):
-            if node == 0 and s == 1:
-                continue
-            j = along(-side * node)
-
-            @pl.when(j < mats)
-            def _():
-                sides = (0, 1) if node == 0 else (s,)
-                last = []
-                for part in range(len(PARTS)):
-                    for t in sides:
-                        reach = PARTS[part][2][t]
-                        if node > reach:
-                            continue
-                        if node > 0:
-                            spread_copy(which, part, t, node, j).wait_recv()
-                        for child in children(node, reach):
-                            copy = spread_copy(which, part, t, child, j)
-                            if children(child, reach):
-                                copy.start()
-                            else:
-                                last.append(copy)
-                for copy in last:
-                    copy.start()
+        for leaf in (False, True):
+            for part in range(len(PARTS)):
+                for s, side in enumerate(SIDES):
+                    reach = PARTS[part][2][s]
+                    targets = [c for c in children(node, reach) if (not children(c, reach)) == leaf]
+                    if node > reach or (leaf and not targets):
+                        continue
+                    j = along(-side * node)
+
+                    @pl.when(held(j))
+                    def _():
+                        if node > 0 and (not leaf or not children(node, reach)):
+                            spread_copy(which, part, s, node, j).wait_recv()
+                        for child in targets:
+                            spread_copy(which, part, s, child, j).start()
 
     def spread_sent(which):
         for node in PARENT:
             for s, side in enumerate(SIDES):
                 j = along(-side * PARENT[node])
 
-                @pl.when(j < mats)
+                @pl.when(held(j))
                 def _():
                     for part in range(len(PARTS)):
                         if node <= PARTS[part][2][s]:
@@ -214,8 +221,8 @@
     def slab_of(ref, index):
         return ref.at[pl.ds(pl.multiple_of(index * slab, slab), slab)]
 
-    def plane_wait(which):
-        view = whole.at[pl.ds(0, short - slab)]
+    def plane_wait(which, count):
+        view = slabs.at[pl.ds(0, count)]
         return plane_copy(view, view, which, lax.rem(me + 1, n_zero))
 
     row_ids = me * shard + lax.broadcasted_iota(jnp.int32, (shard, short), 0)
@@ -240,34 +247,61 @@
             totals.append(total)
         live = live_part(mine)
         gradient = jnp.where(live, jnp.concatenate(totals, axis=0), 0.0)
-        sums[layer] = gradient.astype(BF16)
-        momentum = jnp.where(live, momentum_decay * moms[layer] + gradient, 0.0)
+        sums[mine] = gradient.astype(BF16)
+        momentum = jnp.where(live, momentum_decay * moms[mine] + gradient, 0.0)
         nesterov = (gradient + momentum_decay * momentum).astype(BF16)
         nest[0:shard] = nesterov
         nest[shard:] = jnp.zeros((nest.shape[0] - shard, short), BF16)
-        tall = nest[...]
-        gram[...] = lax.dot_general(tall, tall, (((0,), (0,)), ((), ())), preferred_element_type=F32)
-        for move in plane_moves():
-            peer = beside(move)
-            plane_copy(slab_of(gram, peer), slabs.at[me], 0, peer).start()
-        slabs[me] = slab_of(gram, me)[...]
+        left, right = nest[:, 0:half_short], nest[:, half_short:]
+        for index, (a, b) in enumerate(((left, left), (left, right), (right, right))):
+            gram[pl.ds(index * half_short, half_short)] = lax.dot_general(
+                a, b, (((0,), (0,)), ((), ())), preferred_element_type=F32
+            )
+        for move in chip_moves()[:-1]:
+            chip, peer = adder(move)
+            plane_copy(slab_of(gram, chip), slabs.at[me], 0, peer).start()
+
+        @pl.when(adds)
+        def _():
+            slabs[me] = slab_of(gram, me // 2)[...]
+
+        @pl.when(jnp.logical_not(adds))
+        def _():
+            plane_copy(slab_of(gram, me // 2), slabs.at[me], 0, beside((0, 0, 1))).start()
 
     spread_step(0, 0)
     spread_step(0, 2)
 
     @pl.when(owner)
     def _():
-        plane_wait(0).wait_recv()
-        slab_of(whole, me)[...] = jnp.sum(slabs[...], axis=0)
-        for move in plane_moves():
-            plane_copy(slab_of(whole, me), slab_of(whole, me), 1, beside(move)).start()
+        @pl.when(adds)
+        def _():
+            plane_wait(0, n_zero - 1).wait_recv()
+            mine_of = slab_of(whole, me // 2)
+            mine_of[...] = jnp.sum(slabs[...], axis=0)
+            for y, x in chip_moves():
+                for c in (0, 1):
+                    if (y, x, c) != (0, 0, 0):
+                        plane_copy(mine_of, mine_of, 1, beside((y, x, c))).start()
 
     spread_step(0, 4)
 
     @pl.when(owner)
     def _():
-        plane_wait(1).wait_recv()
-        full = whole[...]
+        chips = n_zero // 2
+
+        @pl.when(adds)
+        def _():
+            plane_wait(1, chips - 1).wait_recv()
+
+        @pl.when(jnp.logical_not(adds))
+        def _():
+            plane_wait(1, chips).wait_recv()
+
+        blocks = [whole[pl.ds(index * half_short, half_short)] for index in range(3)]
+        full = jnp.concatenate(
+            [jnp.concatenate(blocks[0:2], axis=1), jnp.concatenate([blocks[1].T, blocks[2]], axis=1)], axis=0
+        )
         on_diagonal = lax.broadcasted_iota(jnp.int32, (short, short), 0) == lax.broadcasted_iota(
             jnp.int32, (short, short), 1
         )
@@ -307,34 +341,26 @@
         if node == 8:
             j = along(8)
 
-            @pl.when(j < mats)
+            @pl.when(held(j))
             def _():
-                new_momentum(j, sums[j].astype(F32))
+                new_momentum(matrix(j), sums[matrix(j)].astype(F32))
             return
         for s, side in enumerate(SIDES):
             if node == 0 and s == 1:
                 continue
             j = along(-side * node)
 
-            @pl.when(j < mats)
+            @pl.when(held(j))
             def _():
-                new_momentum(j, sums[j].astype(F32))
-
+                new_momentum(matrix(j), sums[matrix(j)].astype(F32))
+
+    spread_step(1, 2)
     spread_step(0, 6)
-    spread_step(0, 1)
-    for node in (0, 1, 2):
-        new_momenta(node)
-    spread_step(1, 2)
-    spread_step(0, 3)
-    for node in (3, 4):
-        new_momenta(node)
     spread_step(1, 4)
-    spread_step(0, 5)
-    for node in (5, 6):
-        new_momenta(node)
     spread_step(1, 6)
-    for node in (7, 8):
+    for node in (1, 3, 5, 7, 8):
         spread_step(0, node)
+    for node in range(9):
         new_momenta(node)
     store_news = pltpu.make_async_copy(news, new_ref, store_sem.at[1])
     store_news.start()
@@ -343,7 +369,7 @@
         for s, side in enumerate(SIDES):
             j = along(side * node)
 
-            @pl.when(j < mats)
+            @pl.when(held(j))
             def _():
                 for part in range(len(PARTS)):
                     if node <= PARTS[part][2][s]:
@@ -353,68 +379,78 @@
 
     @pl.when(owner)
     def _():
-        plane_wait(0).wait_send()
-        plane_wait(1).wait_send()
         keep.wait()
+
+        @pl.when(adds)
+        def _():
+            plane_wait(0, n_zero // 2 - 1).wait_send()
+            plane_wait(1, n_zero - 1).wait_send()
+
+        @pl.when(jnp.logical_not(adds))
+        def _():
+            plane_wait(0, n_zero // 2).wait_send()
 
     for node in (1, 3, 5, 7, 8):
         spread_step(1, node)
+    load_tails = pltpu.make_async_copy(upd_ref.at[:, pl.ds(shard, EXTRA)], tails, load_sem.at[0])
+    load_tails.start()
     spread_sent(1)
-    store_news.wait()
-
-
-def finish(mats, shapes_ref, owners_ref, new_in, upd_in, new_ref, upd_ref, norm_ref, tails, sem):
-    shard, short = new_in.shape[1:]
-    copies = (
-        pltpu.make_async_copy(upd_in.at[:, pl.ds(shard, EXTRA)], tails, sem.at[0]),
-        pltpu.make_async_copy(new_in, new_ref, sem.at[1]),
-        pltpu.make_async_copy(upd_in.at[:, pl.ds(0, shard)], upd_ref, sem.at[2]),
-    )
-    for copy in copies:
-        copy.start()
-    me = lax.axis_index("zero")
-    copies[0].wait()
+    load_tails.wait()
     result = jnp.zeros((1, short), F32)
     for k in range(mats):
         area = (shapes_ref[0, k] * shapes_ref[1, k]).astype(F32)
         norm = jnp.sum(tails[k].astype(F32), axis=0, keepdims=True)
-        held = jnp.full((1, short), owners_ref[k], jnp.int32) == me
-        result = result + jnp.where(held, norm / jnp.sqrt(jnp.full((1, short), area, F32)), 0.0)
-    norm_ref[...] = result[:, 0:1]
-    copies[1].wait()
-    copies[2].wait()
+        kept = jnp.full((1, short), owners_ref[k], jnp.int32) == me
+        result = result + jnp.where(kept, norm / jnp.sqrt(jnp.full((1, short), area, F32)), 0.0)
+    norm_ref[...] = jnp.broadcast_to(result[:, 0 : norm_ref.shape[1]], norm_ref.shape)
+    store_news.wait()
+
+
+def finish(new_in, upd_in, norm_in, new_ref, upd_ref, norm_ref, sem):
+    copies = (
+        pltpu.make_async_copy(new_in, new_ref, sem.at[0]),
+        pltpu.make_async_copy(upd_in.at[:, pl.ds(0, upd_ref.shape[1])], upd_ref, sem.at[1]),
+    )
+    for copy in copies:
+        copy.start()
+    norm_ref[...] = norm_in[0:1, 0:1]
+    for copy in copies:
+        copy.wait()
 
 
 def per_device(n_dp, n_zero, grad_partial, momentum, shapes, owners):
     mats, shard, short = momentum.shape
     smem = pl.BlockSpec(memory_space=pltpu.SMEM)
+    vmem = pl.BlockSpec(memory_space=pltpu.VMEM)
     hbm = pl.BlockSpec(memory_space=pltpu.HBM)
     anywhere = pl.BlockSpec(memory_space=pl.ANY)
     slots = 9
     turned = pltpu.with_memory_space_constraint(shapes.T, pltpu.HBM)
     owners = pltpu.with_memory_space_constraint(owners, pltpu.HBM)
-    new, update = pl.pallas_call(
+    new, update, norms = pl.pallas_call(
         functools.partial(kernel, mats, n_dp, n_zero),
         out_shape=(
             jax.ShapeDtypeStruct((mats, shard, short), F32),
             jax.ShapeDtypeStruct((mats, shard + EXTRA, short), BF16),
+            jax.ShapeDtypeStruct((8, 128), F32),
         ),
-        in_specs=[smem, hbm, hbm],
-        out_specs=(anywhere, anywhere),
+        in_specs=[smem, smem, hbm, hbm],
+        out_specs=(anywhere, anywhere, vmem),
         scratch_shapes=[
             pltpu.VMEM((mats, shard, short), BF16),
             pltpu.VMEM((mats, shard, short), F32),
             pltpu.VMEM((mats, shard, short), BF16),
             pltpu.VMEM((mats, shard, short), F32),
             pltpu.VMEM((shard + EXTRA, short), BF16),
+            pltpu.VMEM((mats, EXTRA, short), BF16),
             pltpu.VMEM((2, slots, PARTS[0][1], short), BF16),
             pltpu.VMEM((2, slots, PARTS[1][1], short), BF16),
             pltpu.VMEM((2, slots, PARTS[0][1], short), BF16),
             pltpu.VMEM((2, slots, PARTS[1][1], short), BF16),
             pltpu.VMEM((128, short), BF16),
-            pltpu.VMEM((short, short), F32),
-            pltpu.VMEM((n_zero, short // n_zero, short), F32),
-            pltpu.VMEM((short, short), F32),
+            pltpu.VMEM((3 * short // 2, short // 2), F32),
+            pltpu.VMEM((n_zero, 3 * short // n_zero, short // 2), F32),
+            pltpu.VMEM((3 * short // 2, short // 2), F32),
             pltpu.SemaphoreType.DMA((2,)),
             pltpu.SemaphoreType.DMA((2,)),
             pltpu.SemaphoreType.REGULAR((4,)),
@@ -428,19 +464,19 @@
         compiler_params=pltpu.CompilerParams(
             collective_id=0, has_side_effects=True, vmem_limit_bytes=24 * 1024 * 1024
         ),
-    )(turned, *(pltpu.with_memory_space_constraint(a, pltpu.HBM) for a in (grad_partial, momentum)))
+    )(turned, owners, *(pltpu.with_memory_space_constraint(a, pltpu.HBM) for a in (grad_partial, momentum)))
     return pl.pallas_call(
-        functools.partial(finish, mats),
+        finish,
         out_shape=(
             jax.ShapeDtypeStruct((mats, shard, short), F32),
             jax.ShapeDtypeStruct((mats, shard, short), BF16),
             jax.ShapeDtypeStruct((1, 1), F32),
         ),
-        in_specs=[smem, smem, anywhere, anywhere],
-        out_specs=(anywhere, anywhere, pl.BlockSpec(memory_space=pltpu.VMEM)),
-        scratch_shapes=[pltpu.VMEM((mats, EXTRA, short), BF16), pltpu.SemaphoreType.DMA((3,))],
+        in_specs=[anywhere, anywhere, vmem],
+        out_specs=(anywhere, anywhere, vmem),
+        scratch_shapes=[pltpu.SemaphoreType.DMA((2,))],
         compiler_params=pltpu.CompilerParams(vmem_limit_bytes=24 * 1024 * 1024),
-    )(turned, owners, new, update)
+    )(new, update, norms)
 
 
 def solution(mesh):

time: 72.2 us -> 69.7 us (0.965)
  Pallas kernels: 70.8 us -> 68.9 us
    pallas_call x1, Pallas kernels: 68.2 us -> 66.9 us  [per_device(): pl.pallas_call(functools.partial(kernel, mats, n_dp, n_zero), out_shape=(...]
where the time goes in v3:
time: 69.7 us; the launch traced here: 69.5 us
  Pallas kernels  68.9 us (99%)
    pallas_call x1, Pallas kernels, per_device(): pl.pallas_call(functools.partial(kernel, mats, n_dp, n_zero), out_shape=(...  66.9 us
    pallas_call x1, Pallas kernels, per_device(): pl.pallas_call(finish, out_shape=(jax.ShapeDtypeStruct((mats, shard, shor...  1.94 us

profile of v3, /device:TPU:1, one launch (start us, length us, event | category | flops | bytes accessed | tf_op | source)
XLA Modules:
  0.0 69.5 jit_solution(15922060280524766323)
XLA Ops:
  0.6 66.9 %shard_map.67 = (f32[14,112,256]{2,1,0:T(8,128)S(1)}, bf16[14,128,256]{2,1,0:T(8,128)(2,1)S(1)}, f32[8,128]{1,0:T(8,128)S(1)}) custom-call(s32[2,14]{1,0:T(2,128)} %bitcast.1, s32[14]{0:T(128)} %owners_ref.1, bf16[1,14,112,256]{3,2,1,0:T(8,128)(2,1)} %grad_ref.1, f32[14,112,256]{2,1,0:T(8,128)} %mom_ref.1), custom_call_target="tpu_custom_call" | custom-call | tf_op jit(solution)/shard_map/pallas_call | solution.py:430
  67.6 1.9 %shard_map.68 = (f32[14,112,256]{2,1,0:T(8,128)}, bf16[14,112,256]{2,1,0:T(8,128)(2,1)}, f32[1,1]{1,0:T(1,128)}) custom-call(f32[14,112,256]{2,1,0:T(8,128)S(1)} %get-tuple-element.6.new_in, bf16[14,128,256]{2,1,0:T(8,128)(2,1)S(1)} %get-tuple-element.7.upd_in, f32[8,128]{1,0:T(8,128)S(1)} %get-tuple-element.8.norm_in), custom_call_target="tpu_custom_call" | custom-call | tf_op jit(solution)/shard_map/pallas_call | solution.py:468

commit v4 on v3

--- a/solution.py
+++ b/solution.py
@@ -21,7 +21,6 @@
 SIDES = (1, -1)
 PARTS = ((0, 64, (8, 7)), (64, 48, (7, 8)))
 SIDE_X, SIDE_Y = 4, 4
-EXTRA = 16
 
 
 def children(node, reach):
@@ -47,7 +46,7 @@
 
 def kernel(
     mats, n_dp, n_zero, shapes_ref, owners_ref, grad_ref, mom_ref, new_ref, upd_ref, norm_ref,
-    grads, moms, sums, news, own, tails, arrived_a, arrived_b, outgoing_a, outgoing_b, nest, gram, slabs, whole,
+    grads, moms, sums, news, own, tiles, arrived, outgoing, nest, gram, slabs, whole,
     load_sem, store_sem, met_sem, rs_send, rs_recv, ag_send, ag_recv, plane_send, plane_recv,
 ):
     layer = lax.axis_index("dp")
@@ -55,7 +54,6 @@
     shard, short = grads.shape[1:]
     half_short = short // 2
     slab = 3 * half_short // (SIDE_X * SIDE_Y)
-    arrived, outgoing = (arrived_a, arrived_b), (outgoing_a, outgoing_b)
     half = n_dp // 2
 
     def held(at):
@@ -114,10 +112,14 @@
 
     meet(0)
 
+    def block(ref, part, *where):
+        first, rows, _ = PARTS[part]
+        return ref.at[*where, pl.ds(first, rows)]
+
     def reduce_copy(part, s, node, source):
         return pltpu.make_async_remote_copy(
             src_ref=source,
-            dst_ref=arrived[part].at[s, node],
+            dst_ref=block(arrived, part, s, node),
             send_sem=rs_send.at[part, s, node],
             recv_sem=rs_recv.at[part, s, node],
             device_id={"dp": along(SIDES[s] * (node - PARENT[node]))},
@@ -125,18 +127,17 @@
         )
 
     def own_rows(part, j):
-        first, rows, _ = PARTS[part]
-        return grads.at[matrix(j), pl.ds(first, rows)]
+        return block(grads, part, matrix(j))
 
     def collected(part, s, node, total):
         for child in reversed(children(node, PARTS[part][2][s])):
-            reduce_copy(part, s, child, arrived[part].at[s, child]).wait_recv()
-            total = total + arrived[part][s, child].astype(F32)
+            reduce_copy(part, s, child, block(arrived, part, s, child)).wait_recv()
+            total = total + block(arrived, part, s, child)[...].astype(F32)
         return total
 
     def reduce_source(part, s, node, j):
         if children(node, PARTS[part][2][s]):
-            return outgoing[part].at[s, node]
+            return block(outgoing, part, s, node)
         return own_rows(part, j)
 
     def reduce_step(node):
@@ -150,7 +151,7 @@
                 def _():
                     if children(node, PARTS[part][2][s]):
                         total = collected(part, s, node, own_rows(part, j)[...].astype(F32))
-                        outgoing[part][s, node] = total.astype(BF16)
+                        block(outgoing, part, s, node)[...] = total.astype(BF16)
                     reduce_copy(part, s, node, reduce_source(part, s, node, j)).start()
 
     for node in (8, 7, 5, 6):
@@ -165,8 +166,6 @@
 
     def spread_copy(which, part, s, node, j):
         first, rows, _ = PARTS[part]
-        if which == 1 and part == len(PARTS) - 1:
-            rows += EXTRA
         window = (sums, upd_ref)[which].at[matrix(j), pl.ds(first, rows)]
         source = window
         if which == 1 and PARENT[node] == 0:
@@ -285,6 +284,7 @@
                         plane_copy(mine_of, mine_of, 1, beside((y, x, c))).start()
 
     spread_step(0, 4)
+    spread_step(0, 6)
 
     @pl.when(owner)
     def _():
@@ -315,20 +315,18 @@
             a_high, a_low = split(a)
             poly = (coef_b * a_high.astype(F32) + coef_c * dot(a_high, a_high)).astype(BF16)
             if sweep < ITERS - 1:
-                half = coef_a * a + dot(a_high, poly) + dot(a_low, poly)
+                both = dot(jnp.concatenate([a_high, a_low, state], axis=0), poly)
+                half = coef_a * a + both[0:short] + both[short : 2 * short]
                 half_high, half_low = split(half)
-                a = coef_a * half + dot(poly, half_high) + dot(poly, half_low)
-            state = (coef_a * state.astype(F32) + dot(state, poly)).astype(BF16)
+                twice = dot(poly, jnp.concatenate([half_high, half_low], axis=1))
+                a = coef_a * half + twice[:, 0:short] + twice[:, short:]
+                moved = both[2 * short :]
+            else:
+                moved = dot(state, poly)
+            state = (coef_a * state.astype(F32) + moved).astype(BF16)
         longest = jnp.maximum(shapes_ref[0, mine], shapes_ref[1, mine]).astype(F32)
         scale = 0.2 * jnp.sqrt(jnp.full((1, 1), longest, F32))
-        own[0:shard] = (state[0:shard].astype(F32) * scale).astype(BF16)
-        one = jnp.broadcast_to(norm, (EXTRA, short))
-        high, rest = split(one)
-        low, rest = split(one - high.astype(F32))
-        place = lax.broadcasted_iota(jnp.int32, (EXTRA, short), 0)
-        own[shard:] = jnp.where(
-            place == 0, high.astype(F32), jnp.where(place == 1, low.astype(F32), jnp.where(place == 2, rest.astype(F32), 0.0))
-        ).astype(BF16)
+        own[...] = (state[0:shard].astype(F32) * scale).astype(BF16)
 
     spread_step(1, 0)
     keep = pltpu.make_async_copy(own, upd_ref.at[mine], store_sem.at[0])
@@ -355,13 +353,23 @@
                 new_momentum(matrix(j), sums[matrix(j)].astype(F32))
 
     spread_step(1, 2)
-    spread_step(0, 6)
-    spread_step(1, 4)
-    spread_step(1, 6)
     for node in (1, 3, 5, 7, 8):
         spread_step(0, node)
     for node in range(9):
         new_momenta(node)
+    lanes = lax.broadcasted_iota(jnp.int32, (8, 128), 1)
+    squares = jnp.zeros((8, 128), F32)
+    for k in range(mats):
+        value = (sums[k].astype(F32) + momentum_decay * news[k]).astype(BF16).astype(F32)
+        total = jnp.sum(jnp.sum(value * value, axis=0, keepdims=True), axis=1, keepdims=True)
+        squares = jnp.where(lanes == k, total, squares)
+    tiles[me] = squares
+    spread_step(1, 4)
+    for y, x in chip_moves():
+        for c in (0, 1):
+            if (y, x, c) != (0, 0, 0):
+                plane_copy(tiles.at[me], tiles.at[me], 2, beside((y, x, c))).start()
+    spread_step(1, 6)
     store_news = pltpu.make_async_copy(news, new_ref, store_sem.at[1])
     store_news.start()
 
@@ -392,24 +400,25 @@
 
     for node in (1, 3, 5, 7, 8):
         spread_step(1, node)
-    load_tails = pltpu.make_async_copy(upd_ref.at[:, pl.ds(shard, EXTRA)], tails, load_sem.at[0])
-    load_tails.start()
+    tile_view = tiles.at[pl.ds(0, n_zero - 1)]
+    tile_wait = plane_copy(tile_view, tile_view, 2, lax.rem(me + 1, n_zero))
+    tile_wait.wait_recv()
+    norms = jnp.sqrt(jnp.sum(tiles[...], axis=0))
+    result = jnp.zeros((8, 128), F32)
+    for k in range(mats):
+        area = jnp.full((8, 128), (shapes_ref[0, k] * shapes_ref[1, k]).astype(F32), F32)
+        kept = (jnp.full((8, 128), owners_ref[k], jnp.int32) == me) & (lanes == k)
+        result = jnp.where(kept, norms / jnp.sqrt(area), result)
+    norm_ref[...] = jnp.broadcast_to(jnp.sum(result, axis=1, keepdims=True), norm_ref.shape)
+    tile_wait.wait_send()
     spread_sent(1)
-    load_tails.wait()
-    result = jnp.zeros((1, short), F32)
-    for k in range(mats):
-        area = (shapes_ref[0, k] * shapes_ref[1, k]).astype(F32)
-        norm = jnp.sum(tails[k].astype(F32), axis=0, keepdims=True)
-        kept = jnp.full((1, short), owners_ref[k], jnp.int32) == me
-        result = result + jnp.where(kept, norm / jnp.sqrt(jnp.full((1, short), area, F32)), 0.0)
-    norm_ref[...] = jnp.broadcast_to(result[:, 0 : norm_ref.shape[1]], norm_ref.shape)
     store_news.wait()
 
 
 def finish(new_in, upd_in, norm_in, new_ref, upd_ref, norm_ref, sem):
     copies = (
         pltpu.make_async_copy(new_in, new_ref, sem.at[0]),
-        pltpu.make_async_copy(upd_in.at[:, pl.ds(0, upd_ref.shape[1])], upd_ref, sem.at[1]),
+        pltpu.make_async_copy(upd_in, upd_ref, sem.at[1]),
     )
     for copy in copies:
         copy.start()
@@ -431,7 +440,7 @@
         functools.partial(kernel, mats, n_dp, n_zero),
         out_shape=(
             jax.ShapeDtypeStruct((mats, shard, short), F32),
-            jax.ShapeDtypeStruct((mats, shard + EXTRA, short), BF16),
+            jax.ShapeDtypeStruct((mats, shard, short), BF16),
             jax.ShapeDtypeStruct((8, 128), F32),
         ),
         in_specs=[smem, smem, hbm, hbm],
@@ -441,12 +450,10 @@
             pltpu.VMEM((mats, shard, short), F32),
             pltpu.VMEM((mats, shard, short), BF16),
             pltpu.VMEM((mats, shard, short), F32),
-            pltpu.VMEM((shard + EXTRA, short), BF16),
-            pltpu.VMEM((mats, EXTRA, short), BF16),
-            pltpu.VMEM((2, slots, PARTS[0][1], short), BF16),
-            pltpu.VMEM((2, slots, PARTS[1][1], short), BF16),
-            pltpu.VMEM((2, slots, PARTS[0][1], short), BF16),
-            pltpu.VMEM((2, slots, PARTS[1][1], short), BF16),
+            pltpu.VMEM((shard, short), BF16),
+            pltpu.VMEM((n_zero, 8, 128), F32),
+            pltpu.VMEM((2, slots, shard, short), BF16),
+            pltpu.VMEM((2, slots, shard, short), BF16),
             pltpu.VMEM((128, short), BF16),
             pltpu.VMEM((3 * short // 2, short // 2), F32),
             pltpu.VMEM((n_zero, 3 * short // n_zero, short // 2), F32),
@@ -458,8 +465,8 @@
             pltpu.SemaphoreType.DMA((len(PARTS), 2, slots)),
             pltpu.SemaphoreType.DMA((2, len(PARTS), 2, slots)),
             pltpu.SemaphoreType.DMA((2, len(PARTS), 2, slots)),
-            pltpu.SemaphoreType.DMA((2,)),
-            pltpu.SemaphoreType.DMA((2,)),
+            pltpu.SemaphoreType.DMA((3,)),
+            pltpu.SemaphoreType.DMA((3,)),
         ],
         compiler_params=pltpu.CompilerParams(
             collective_id=0, has_side_effects=True, vmem_limit_bytes=24 * 1024 * 1024

time: 69.7 us -> 68.8 us (0.987)
  Pallas kernels: 68.9 us -> 68 us
    pallas_call x1, Pallas kernels: 66.9 us -> 66.1 us  [per_device(): pl.pallas_call(functools.partial(kernel, mats, n_dp, n_zero), out_shape=(...]
where the time goes in v4:
time: 68.8 us; the launch traced here: 68.6 us
  Pallas kernels  68 us (99%)
    pallas_call x1, Pallas kernels, per_device(): pl.pallas_call(functools.partial(kernel, mats, n_dp, n_zero), out_shape=(...  66.1 us
    pallas_call x1, Pallas kernels, per_device(): pl.pallas_call(finish, out_shape=(jax.ShapeDtypeStruct((mats, shard, shor...  1.94 us

profile of v4, /device:TPU:1, one launch (start us, length us, event | category | flops | bytes accessed | tf_op | source)
XLA Modules:
  0.0 68.6 jit_solution(6250593314742305899)
XLA Ops:
  0.6 66.1 %shard_map.67 = (f32[14,112,256]{2,1,0:T(8,128)S(1)}, bf16[14,112,256]{2,1,0:T(8,128)(2,1)S(1)}, f32[8,128]{1,0:T(8,128)S(1)}) custom-call(s32[2,14]{1,0:T(2,128)} %bitcast.1, s32[14]{0:T(128)} %owners_ref.1, bf16[1,14,112,256]{3,2,1,0:T(8,128)(2,1)} %grad_ref.1, f32[14,112,256]{2,1,0:T(8,128)} %mom_ref.1), custom_call_target="tpu_custom_call" | custom-call | tf_op jit(solution)/shard_map/pallas_call | solution.py:439
  66.7 1.9 %shard_map.68 = (f32[14,112,256]{2,1,0:T(8,128)}, bf16[14,112,256]{2,1,0:T(8,128)(2,1)}, f32[1,1]{1,0:T(1,128)}) custom-call(f32[14,112,256]{2,1,0:T(8,128)S(1)} %get-tuple-element.6.new_in, bf16[14,112,256]{2,1,0:T(8,128)(2,1)S(1)} %get-tuple-element.7.upd_in, f32[8,128]{1,0:T(8,128)S(1)} %get-tuple-element.8.norm_in), custom_call_target="tpu_custom_call" | custom-call | tf_op jit(solution)/shard_map/pallas_call | solution.py:475

commit v5 on v4

--- a/solution.py
+++ b/solution.py
@@ -140,8 +140,8 @@
             return block(outgoing, part, s, node)
         return own_rows(part, j)
 
-    def reduce_step(node):
-        for part in range(len(PARTS)):
+    def reduce_step(node, parts=tuple(range(len(PARTS)))):
+        for part in parts:
             for s, side in enumerate(SIDES):
                 if node > PARTS[part][2][s]:
                     continue
@@ -154,7 +154,10 @@
                         block(outgoing, part, s, node)[...] = total.astype(BF16)
                     reduce_copy(part, s, node, reduce_source(part, s, node, j)).start()
 
-    for node in (8, 7, 5, 6):
+    for part in range(len(PARTS)):
+        for node in (8, 7):
+            reduce_step(node, (part,))
+    for node in (5, 6):
         reduce_step(node)
     meet(1)
     for node in (3, 4):

time: 68.8 us -> 69.2 us (level)
  no operation moved by 1% of the time
where the time goes in v5:
time: 69.2 us; the launch traced here: 69 us
  Pallas kernels  68.4 us (99%)
    pallas_call x1, Pallas kernels, per_device(): pl.pallas_call(functools.partial(kernel, mats, n_dp, n_zero), out_shape=(...  66.4 us
    pallas_call x1, Pallas kernels, per_device(): pl.pallas_call(finish, out_shape=(jax.ShapeDtypeStruct((mats, shard, shor...  1.94 us

profile of v5, /device:TPU:1, one launch (start us, length us, event | category | flops | bytes accessed | tf_op | source)
XLA Modules:
  0.0 69.0 jit_solution(4497618869798825926)
XLA Ops:
  0.6 66.4 %shard_map.67 = (f32[14,112,256]{2,1,0:T(8,128)S(1)}, bf16[14,112,256]{2,1,0:T(8,128)(2,1)S(1)}, f32[8,128]{1,0:T(8,128)S(1)}) custom-call(s32[2,14]{1,0:T(2,128)} %bitcast.1, s32[14]{0:T(128)} %owners_ref.1, bf16[1,14,112,256]{3,2,1,0:T(8,128)(2,1)} %grad_ref.1, f32[14,112,256]{2,1,0:T(8,128)} %mom_ref.1), custom_call_target="tpu_custom_call" | custom-call | tf_op jit(solution)/shard_map/pallas_call | solution.py:442
  67.1 1.9 %shard_map.68 = (f32[14,112,256]{2,1,0:T(8,128)}, bf16[14,112,256]{2,1,0:T(8,128)(2,1)}, f32[1,1]{1,0:T(1,128)}) custom-call(f32[14,112,256]{2,1,0:T(8,128)S(1)} %get-tuple-element.6.new_in, bf16[14,112,256]{2,1,0:T(8,128)(2,1)S(1)} %get-tuple-element.7.upd_in, f32[8,128]{1,0:T(8,128)S(1)} %get-tuple-element.8.norm_in), custom_call_target="tpu_custom_call" | custom-call | tf_op jit(solution)/shard_map/pallas_call | solution.py:478
